TPU v7x, 512 devices: a whole 4x4x16 slice. The times are simulated.
512 devices in a mesh: head: 8 (over z_hi, core), batch: 64 (over y, x, z_lo).
Axes of the slice: x: 4, y: 4, z: 16 (z_hi: 4, z_lo: 4; z = z_hi * 4 + z_lo), core: 2. Of those that a mesh axis runs over, the one named last changes fastest.
Arguments:
- prompt_kv: bfloat16 [64, 1024, 2048], P(None, ('head', 'batch')), may hold values from -6 to 6
- prompt_lengths: int32 [64], replicated, may hold values from 128 to 1024, as said below
- owner_prompts: int32 [64, 2], replicated, may hold values from 0 to 63, as said below
- owner_counts: int32 [64], P('batch'), may hold values from 0 to 32, as said below
- queries: bfloat16 [2048, 4, 8192], P('batch', None, 'head'), may hold values from -40 to 40
- new_kv: bfloat16 [2048, 4, 2048], P('batch', None, 'head'), may hold values from -6 to 6
Outputs:
- attention: bfloat16 [2048, 4, 8192], P('batch', None, 'head')
Inputs may be any that keep to these rules, and one draw needn't show every extreme that they name: `prompt_lengths`: some prompt has each end of the range as its length. `owner_prompts`: the first owner_counts[o] / 16 entries of row o are live and, over all rows, the live entries name every prompt exactly once; other entries are arbitrary prompt ids. `owner_counts`: multiples of 16 that sum to 1024; some owner holds 32 samples.
All inputs are finite; a program needn't handle non-finite values.
Results may differ from a plain program's by a relative error of at most 0.003.
Values may be sent and summed in bfloat16 or wider, within the bound.
A program may use at most 64 MiB of HBM per device.

v0:
```python
import math

import jax
import jax.numpy as jnp
from jax import lax
from jax.sharding import PartitionSpec as P

HD = 128
QH = 64
KVH = 8
GROUP = 16
STEPS = 4


def local(prompt_kv, prompt_lengths, owner_prompts, owner_counts, queries, new_kv):
    owner_index = lax.axis_index("batch")
    owners = lax.axis_size("batch")
    groups_held = owner_prompts.shape[1]
    ctx_local = prompt_kv.shape[1]
    kv_local = new_kv.shape[2] // (2 * HD)
    per_kv = QH // KVH
    scale = 1.0 / math.sqrt(HD)
    outgoing = jnp.take(prompt_kv, owner_prompts, axis=0)
    regrouped = lax.all_to_all(outgoing, "head", split_axis=3, concat_axis=2, tiled=True)
    arrived = lax.all_to_all(regrouped, "batch", split_axis=0, concat_axis=2, tiled=True)
    total_rows = arrived.shape[2]
    per_source = total_rows // owners
    flat_rows = jnp.arange(total_rows, dtype=jnp.int32)
    source_owner = flat_rows // per_source
    within = flat_rows % per_source
    positions = (within // ctx_local * owners + source_owner) * ctx_local + within % ctx_local
    held = lax.dynamic_index_in_dim(owner_prompts, owner_index, 0, keepdims=False)
    prompt_ids = jnp.arange(prompt_lengths.shape[0], dtype=jnp.int32)
    held_lengths = jnp.sum(
        jnp.where(held[:, None] == prompt_ids[None, :], prompt_lengths[None, :], 0), axis=1
    )
    queries_six = queries.reshape(groups_held, GROUP, STEPS, kv_local, per_kv, HD)
    own_rows = new_kv.reshape(groups_held, GROUP, STEPS, kv_local, 2, HD)
    own_scores = (
        jnp.einsum(
            "kgtjqd,kgujd->kgtjqu",
            queries_six,
            own_rows[:, :, :, :, 0, :],
            preferred_element_type=jnp.float32,
        )
        * scale
    )
    causal = jnp.arange(STEPS)[None, :] <= jnp.arange(STEPS)[:, None]
    own_scores = jnp.where(causal[None, None, :, None, None, :], own_scores, -jnp.inf)
    start_top = jnp.max(own_scores, axis=-1)
    own_exps = jnp.exp(own_scores - start_top[..., None])
    start_sum = jnp.sum(own_exps, axis=-1)
    start_acc = jnp.einsum(
        "kgtjqu,kgujd->kgtjqd",
        own_exps.astype(jnp.bfloat16),
        own_rows[:, :, :, :, 1, :],
        preferred_element_type=jnp.float32,
    )
    block_rows = min(1024, total_rows)
    block_count = total_rows // block_rows
    keys_view = arrived[0].reshape(groups_held, total_rows, kv_local, 2, HD)

    def step_block(index, carry):
        top, denom, accum = carry
        scores = (
            jnp.einsum(
                "kgtjqd,knjd->kgtjqn",
                queries_six,
                keys_view[:, :, :, 0, :],
                preferred_element_type=jnp.float32,
            )
            * scale
        )
        valid = positions[None, :] < held_lengths[:, None]
        scores = jnp.where(valid[:, None, None, None, None, :], scores, -jnp.inf)
        new_top = jnp.maximum(top, jnp.max(scores, axis=-1))
        factor = jnp.exp(top - new_top)
        exps = jnp.exp(scores - new_top[..., None])
        denom = denom * factor + jnp.sum(exps, axis=-1)
        accum = accum * factor[..., None] + jnp.einsum(
            "kgtjqn,knjd->kgtjqd",
            exps.astype(jnp.bfloat16),
            keys_view[:, :, :, 1, :],
            preferred_element_type=jnp.float32,
        )
        return (new_top, denom, accum)

    top, denom, accum = lax.fori_loop(0, block_count, step_block, (start_top, start_sum, start_acc))
    result = accum / denom[..., None]
    slot_ids = jnp.arange(groups_held * GROUP, dtype=jnp.int32).reshape(groups_held, GROUP)
    live = slot_ids < owner_counts[0]
    result = jnp.where(live[:, :, None, None, None, None], result, 0.0)
    return result.reshape(queries.shape).astype(jnp.bfloat16)


def solution(mesh):
    return jax.shard_map(
        local,
        mesh=mesh,
        in_specs=(
            P(None, ("head", "batch"), None),
            P(),
            P(),
            P("batch"),
            P("batch", None, "head"),
            P("batch", None, "head"),
        ),
        out_specs=P("batch", None, "head"),
        check_vma=False,
    )
```

profile of v0, /device:TPU:1, one launch (start us, length us, event | category | flops | bytes accessed | tf_op | source)
XLA Modules:
  0.0 139.4 jit_solution(5535633865499625291)
XLA Ops:
  0.0 0.7 compare_select_fusion
  0.7 0.7 compare_and_fusion
  1.4 0.1 copy.105
  1.5 0.1 reshape.224
  1.7 0.1 copy.104
  1.8 2.7 %gather_fusion = bf16[128,2,2048]{2,1,0:T(2,128)(2,1)S(1)} fusion(bf16[64,2,2048]{2,1,0:T(2,128)(2,1)S(1)} %copy-done, s32[1024]{0:T(1024)S(1)} %pad_clamp_fusion), kind=kCustom, calls=%fused_computation | custom fusion | bytes 2097664 | tf_op jit(solution)/shard_map/jit(_take)/gather | solution.py:23
  4.5 2.1 %broadcast_select_fusion = bf16[64,2,2,2048]{3,2,1,0:T(2,128)(2,1)} fusion(bf16[64,2,2,2048]{3,2,1,0:T(2,128)(2,1)S(1)} %bitcast.112, pred[64,2]{1,0:T(8,128)(4,1)S(1)} %copy.104), kind=kLoop, calls=%fused_computation.10 | loop fusion | flops 524288 | bytes 2097280 | tf_op jit(solution)/shard_map/jit(_take)/select_n | solution.py:23
  6.5 4.9 %copy.106 = bf16[64,2,2,2048]{0,2,1,3:T(2,128)(2,1)S(1)} copy(bf16[64,2,2,2048]{3,2,1,0:T(2,128)(2,1)} %broadcast_select_fusion) | data formatting | bytes 2097152 | tf_op jit(solution)/shard_map/jit(_take)/select_n | solution.py:23
  11.4 2.7 %reshape.241 = bf16[8,2,32768]{2,1,0:T(2,128)(2,1)} reshape(bf16[2048,2,2,64]{3,2,1,0:T(2,128)(2,1)S(1)} %bitcast.108) | data formatting | bytes 2097152
  14.1 66.7 %all_to_all.33 = bf16[8,2,32768]{2,1,0:T(2,128)(2,1)} all-to-all(bf16[8,2,32768]{2,1,0:T(2,128)(2,1)} %reshape.241), channel_id=1, replica_groups=mesh['head'=8,'batch'=64] {'head'}, dimensions={0} | all-to-all | bytes 2097152 | tf_op jit(solution)/shard_map/all_to_all | solution.py:24
  80.8 3.1 %reshape.242 = bf16[2048,2,2,64]{3,2,1,0:T(2,128)(2,1)S(1)} reshape(bf16[8,2,32768]{2,1,0:T(2,128)(2,1)} %all_to_all.33) | data formatting | bytes 2097152
  83.9 4.2 %copy.130 = bf16[64,2,2,8,256]{4,0,2,3,1:T(8,128)(2,1)} copy(bf16[64,2,2,8,256]{0,2,1,4,3:T(2,128)(2,1)S(1)} %bitcast.109) | data formatting | bytes 2097152 | tf_op jit(solution)/shard_map/all_to_all | solution.py:24
  88.1 2.8 %copy.109 = bf16[64,2,16,256]{3,2,1,0:T(8,128)(2,1)} copy(bf16[64,2,16,256]{3,0,2,1:T(8,128)(2,1)} %bitcast.110) | data formatting | bytes 2097152 | tf_op jit(solution)/shard_map/all_to_all | solution.py:24
  91.0 12.1 %all-to-all-start.1 = ((bf16[64,2,16,256]{3,2,1,0:T(8,128)(2,1)}), bf16[64,2,16,256]{3,2,1,0:T(8,128)(2,1)S(1)}, u32[]{:S(2)}, u32[]{:S(2)}) async-start(bf16[64,2,16,256]{3,2,1,0:T(8,128)(2,1)} %copy.109), calls=%async_computation.1 | async-start | bytes 2097152 | tf_op jit(solution)/shard_map/all_to_all | solution.py:25
  103.1 0.2 dynamic-slice_reduce_fusion
  103.3 0.1 reshape.216
  103.5 0.1 fusion.52
  103.6 1.3 fusion.53
  104.9 0.1 copy.114
  104.9 0.3 fusion.27
  105.2 0.1 copy.118
  106.0 0.2 fusion.50
  106.2 24.4 %all-to-all-done.1 = bf16[64,2,16,256]{3,2,1,0:T(8,128)(2,1)S(1)} async-done(((bf16[64,2,16,256]{3,2,1,0:T(8,128)(2,1)}), bf16[64,2,16,256]{3,2,1,0:T(8,128)(2,1)S(1)}, u32[]{:S(2)}, u32[]{:S(2)}) %all-to-all-start.1) | async-done | bytes 1048608 | tf_op jit(solution)/shard_map/all_to_all | solution.py:25
  130.8 0.3 reshape_squeeze.3
  131.1 2.3 %fusion.51 = (bf16[2,1024,1,1,128]{4,3,1,0,2:T(2,128)(2,1)}, bf16[2,1024,1,1,128]{4,3,1,0,2:T(2,128)(2,1)S(1)}) fusion(bf16[2,1024,1,2,128]{4,3,1,0,2:T(2,128)(2,1)S(1)} %reshape_squeeze.3), kind=kLoop, calls=%fused_computation.71 | loop fusion | bytes 2097152 | tf_op jit(solution)/shard_map/while/body/eval_jaxpr/slice | solution.py:83
  133.4 0.9 bitcast_reduce_fusion
  134.2 1.1 fusion.3
  135.3 0.1 copy.115
  135.4 0.1 copy.119
  135.5 0.4 fusion.19
  135.9 2.7 %fusion.20 = bf16[2,16,4,1,8,128]{5,4,2,1,0,3:T(8,128)(2,1)S(1)} fusion(f32[2,16,4,1,8,128]{5,4,2,1,0,3:T(8,128)S(1)} %fusion.19, bf16[2,16,4,8,1024]{4,1,3,2,0:T(8,128)(2,1)S(1)} %get-tuple-element.21, bf16[2,1024,1,1,128]{4,3,1,0,2:T(2,128)(2,1)} %get-tuple-element.23, f32[2,16,4,8]{3,2,1,0:T(4,128)S(1)} %copy.119, pred[2,16]{1,0:T(4,128)(4,1)S(1)} %add_compare_fusion), kind=kOutput, calls=%fused_computation.18 | convolution fusion | flops 268959744 | bytes 3412000 | tf_op jit(solution)/shard_map/while/body/eval_jaxpr/kgtjqn,knjd->kgtjqd/dot_general | solution.py:80
  138.6 0.8 convert_element_type.16
  (19 shorter events, 0.3 us)
Async XLA Ops:
  0.0 1.8 %copy-start = (bf16[64,2,2048]{2,1,0:T(2,128)(2,1)S(1)}, bf16[64,2,2048]{2,1,0:T(2,128)(2,1)}, u32[]{:S(2)}) copy-start(bf16[64,2,2048]{2,1,0:T(2,128)(2,1)} %param.6) | copy-start | bytes 1572868
  83.9 19.2 %copy-start.3 = (s32[64,2]{0,1:T(2,128)S(1)}, s32[64,2]{0,1:T(2,128)}, u32[]{:S(2)}) copy-start(s32[64,2]{0,1:T(2,128)} %param.8) | copy-start | bytes 1540
  83.9 19.4 %copy-start.1 = (bf16[32,4,1024]{2,1,0:T(4,128)(2,1)S(1)}, bf16[32,4,1024]{2,1,0:T(4,128)(2,1)}, u32[]{:S(2)}) copy-start(bf16[32,4,1024]{2,1,0:T(4,128)(2,1)} %param.10) | copy-start | bytes 786436
  83.9 19.5 %copy-start.2 = (bf16[32,4,256]{2,1,0:T(4,128)(2,1)S(1)}, bf16[32,4,256]{2,1,0:T(4,128)(2,1)}, u32[]{:S(2)}) copy-start(bf16[32,4,256]{2,1,0:T(4,128)(2,1)} %param.11) | copy-start | bytes 196612
  83.9 22.0 %copy-start.4 = (s32[64]{0:T(128)S(1)}, s32[64]{0:T(128)}, u32[]{:S(2)}) copy-start(s32[64]{0:T(128)} %param.7) | copy-start | bytes 772
  91.0 39.7 %all-to-all-start.1 = ((bf16[64,2,16,256]{3,2,1,0:T(8,128)(2,1)}), bf16[64,2,16,256]{3,2,1,0:T(8,128)(2,1)S(1)}, u32[]{:S(2)}, u32[]{:S(2)}) async-start(bf16[64,2,16,256]{3,2,1,0:T(8,128)(2,1)} %copy.109), calls=%async_computation.1 | async-start | bytes 2097152 | tf_op jit(solution)/shard_map/all_to_all | solution.py:25
where the time goes:
time: 140 us; the launch traced here: 139 us
  blocking collectives  66.7 us (48%)
  local copies, waits for them, and re-layouts  24.9 us (18%)
  waiting for transfers between devices  24.4 us (17%)
  starting transfers between devices  12.1 us (9%)
  matrix products  5.21 us (4%)
  other arithmetic  5.11 us (4%)
    all_to_all x1, blocking collectives, local(): lax.all_to_all(outgoing, 'head', split_axis=3, concat_axis=2, tiled=True)  66.7 us
    all_to_all x1, waiting for transfers between devices, local(): lax.all_to_all(regrouped, 'batch', split_axis=0, concat_axis=2, tiled=True)  24.4 us
    all_to_all x1, starting transfers between devices, local(): lax.all_to_all(regrouped, 'batch', split_axis=0, concat_axis=2, tiled=True)  12.1 us
    all_to_all x2, local copies, waits for them, and re-layouts, local(): lax.all_to_all(outgoing, 'head', split_axis=3, concat_axis=2, tiled=True)  7.02 us
    unnamed x12, local copies, waits for them, and re-layouts  5.79 us
    select_n x2, local copies, waits for them, and re-layouts, local(): outgoing = jnp.take(prompt_kv, owner_prompts, axis=0)  4.98 us
  transfers between devices with their start and end apart: 1, of which 1 were waited for; matrix products, arithmetic and copies ran while one was open for 2% of the time, Pallas kernels for 0%

commit v1 on v0

v1 whole, which is shorter than its diff:
```python
import math

import jax
import jax.numpy as jnp
from jax import lax
from jax.experimental import pallas as pl
from jax.experimental.pallas import tpu as pltpu
from jax.sharding import PartitionSpec as P

HD = 128
GROUP = 16
STEPS = 4
PER_KV = 8
HEADS = 8
PROMPTS = 64
SLOTS = 2
OWNERS = 64
RUNS = 4
POS = 2
MESH = pl.DeviceIdType.MESH
LOWEST = -1e30
SCALE = math.log2(math.e) / math.sqrt(HD)


def iota(shape, dim):
    return lax.broadcasted_iota(jnp.int32, shape, dim)


def place():
    head, batch = lax.axis_index("head"), lax.axis_index("batch")
    return head // 2, head % 2, batch // 4, batch % 4


def device(run, core, yx, node):
    return (lax.rem(run + RUNS, RUNS) * 2 + core, yx * 4 + node)


def relay_of(hop):
    run, _, _, node = place()
    odd, upper = node % 2, node // 2 == 1
    if hop == 1:
        return jnp.where(upper, run + 1, run + 3), jnp.where(upper, odd, 2 + odd)
    if hop == 2:
        return jnp.where(upper, run + 3, run + 1), jnp.where(upper, 2 + odd, odd)
    return run + 2, jnp.where(upper, odd, 2 + odd)


def source_of(hop, run, node):
    odd, upper = node % 2, node // 2 == 1
    if hop == 0:
        return run + 0 * node, node
    if hop == 1:
        return jnp.where(upper, run + 1, run + 3), jnp.where(upper, odd, 2 + odd)
    if hop == 2:
        return jnp.where(upper, run + 1, run + 3), jnp.where(upper, 2 + odd, odd)
    return run + 2, jnp.where(upper, odd, 2 + odd)


def kernel(lengths, prompts, counts, prompts_v, kv_hbm, q_hbm, new_hbm, out_ref,
           kv, q, new, wide, send, land, picked, got, pick, sort, qt, top, total, acc,
           in_sem, s1, r1, s2, r2):
    run, core, yx, node = place()
    me_head, me = lax.axis_index("head"), lax.axis_index("batch")

    loads = [pltpu.make_async_copy(a, b, in_sem.at[i]) for i, (a, b) in enumerate(((kv_hbm, kv), (q_hbm, q), (new_hbm, new)))]
    for load in loads:
        load.start()

    barrier = pltpu.get_barrier_semaphore()
    for hop in (3, 2, 1):
        their_run, their_node = source_of(hop, run, node)
        for k in (0, 1):
            pl.semaphore_signal(barrier, inc=1, device_id=device(their_run, k, yx, their_node), device_id_type=MESH)
    pl.semaphore_signal(barrier, inc=1, device_id=device(run, 1 - core, yx, node), device_id_type=MESH)

    @pl.loop(1, OWNERS)
    def _(i):
        pl.semaphore_signal(barrier, inc=1, device_id=(me_head, lax.rem(me + i, OWNERS)), device_id_type=MESH)

    loads[0].wait()
    for p in range(PROMPTS):
        wide[POS * p : POS * (p + 1), :] = kv[p].astype(jnp.float32)
    for h in range(HEADS):
        send[h] = wide[:, h * 256 : (h + 1) * 256].astype(jnp.bfloat16)

    rows, cols = OWNERS * 8, 2 * PROMPTS * POS
    owner_hot = (iota((rows, OWNERS), 0) // 8 == iota((rows, OWNERS), 1)).astype(jnp.bfloat16)
    ids = jnp.dot(owner_hot, prompts_v[...].astype(jnp.float32).astype(jnp.bfloat16), preferred_element_type=jnp.float32)
    r1d = iota((rows, 1), 0)
    ids = jnp.where(r1d // 4 % 2 == 0, ids[:, 0:1], ids[:, 1:2]).astype(jnp.int32)
    want = (r1d // 2 % 2) * (PROMPTS * POS) + ids * POS + r1d % 2
    pick[...] = (want == iota((rows, cols), 1)).astype(jnp.bfloat16)

    pl.semaphore_wait(barrier, 7 + OWNERS - 1)

    own = pltpu.make_async_copy(send.at[me_head], land.at[0, core], r1.at[0])
    own.start()
    first = []
    first.append(pltpu.make_async_remote_copy(
        send.at[run * 2 + 1 - core], land.at[0, core], s1.at[0], r1.at[0],
        device_id=device(run, 1 - core, yx, node), device_id_type=MESH))
    for hop in (1, 2, 3):
        to_run, to_node = relay_of(hop)
        for k in (0, 1):
            to = device(to_run, k, yx, to_node)
            first.append(pltpu.make_async_remote_copy(
                send.at[to[0]], land.at[hop, core], s1.at[2 * hop - 1 + k], r1.at[hop], device_id=to, device_id_type=MESH))
    for copy in first:
        copy.start()

    def relay(g):
        pltpu.make_async_copy(land.at[g], land.at[g], r1.at[g]).wait()
        found = jnp.dot(pick[...], land[g].reshape(cols, 256), preferred_element_type=jnp.float32)
        keys, values = found[:, :HD].reshape(OWNERS, 8, HD), found[:, HD:].reshape(OWNERS, 8, HD)
        picked[g] = jnp.concatenate([keys, values], axis=1).astype(jnp.bfloat16)
        pltpu.make_async_copy(picked.at[g, me], got.at[g, me], r2.at[g]).start()

        @pl.loop(1, OWNERS)
        def _(i):
            to = lax.rem(me + i, OWNERS)
            pltpu.make_async_remote_copy(
                picked.at[g, to], got.at[g, me], s2.at[g], r2.at[g],
                device_id=(me_head, to), device_id_type=MESH).start()

    relay(0)

    loads[1].wait()
    loads[2].wait()
    for g in range(GROUP * SLOTS):
        wide[STEPS * g : STEPS * (g + 1), :1024] = q[g].astype(jnp.float32)
        wide[STEPS * g : STEPS * (g + 1), 1024:1280] = new[g].astype(jnp.float32)
    side = 64
    rows = PER_KV * side
    for s in range(SLOTS):
        part = wide[side * s : side * (s + 1), :1024].astype(jnp.bfloat16)
        flat = jnp.concatenate([part[:, i * HD : (i + 1) * HD] for i in range(PER_KV)], axis=0)
        qt[s] = flat.astype(jnp.float32).T.astype(jnp.bfloat16)
        mine = wide[side * s : side * (s + 1), 1024:1280].astype(jnp.bfloat16)
        scores = jnp.dot(mine[:, :HD], qt[s], preferred_element_type=jnp.float32) * SCALE
        key, query = iota((side, rows), 0), iota((side, rows), 1) % side
        seen = (key // STEPS == query // STEPS) & (key % STEPS <= query % STEPS)
        scores = jnp.where(seen, scores, LOWEST)
        m = jnp.max(scores, axis=0, keepdims=True)
        e = jnp.where(seen, jnp.exp2(scores - m), 0.0)
        top[s : s + 1, :] = m
        total[s : s + 1, :] = jnp.sum(e, axis=0, keepdims=True)
        acc[s] = lax.dot_general(mine[:, HD:], e.astype(jnp.bfloat16), (((0,), (0,)), ((), ())), preferred_element_type=jnp.float32)

    r, c = iota((256, 256), 0), iota((256, 256), 1)
    sort[...] = (c == (r // 4 % 16) * 16 + (r // 64) * 4 + r % 4).astype(jnp.bfloat16)

    relay(1)
    relay(2)
    relay(3)

    def attend(g):
        pltpu.make_async_copy(got.at[g], got.at[g], r2.at[g]).wait()
        flat = got[g].reshape(OWNERS * 16, HD)
        blocks = [
            jnp.dot(sort[...], flat[256 * i : 256 * (i + 1)], preferred_element_type=jnp.float32).astype(jnp.bfloat16)
            for i in range(4)
        ]
        n = iota((256, rows), 0)
        relay_id = n // 4
        from_run, from_node = source_of(g, run, relay_id % 4)
        from_head = lax.rem(from_run + RUNS, RUNS) * 2 + n // 2 % 2
        position = (from_head * OWNERS + relay_id // 4 * 4 + from_node) * POS + n % 2
        for s in range(SLOTS):
            keys = jnp.concatenate([b[64 * s : 64 * (s + 1)] for b in blocks], axis=0)
            values = jnp.concatenate([b[128 + 64 * s : 128 + 64 * (s + 1)] for b in blocks], axis=0)
            scores = jnp.dot(keys, qt[s], preferred_element_type=jnp.float32) * SCALE
            scores = jnp.where(position < lengths[prompts[me, s]], scores, LOWEST)
            before = top[s : s + 1, :]
            m = jnp.maximum(before, jnp.max(scores, axis=0, keepdims=True))
            e = jnp.exp2(scores - m)
            fade = jnp.exp2(before - m)
            top[s : s + 1, :] = m
            total[s : s + 1, :] = total[s : s + 1, :] * fade + jnp.sum(e, axis=0, keepdims=True)
            acc[s] = acc[s] * fade + lax.dot_general(
                values, e.astype(jnp.bfloat16), (((0,), (0,)), ((), ())), preferred_element_type=jnp.float32)

    for g in range(4):
        attend(g)

    for s in range(SLOTS):
        live = s * GROUP < counts[0]
        result = jnp.where(live, acc[s] / total[s : s + 1, :], 0.0).T.astype(jnp.bfloat16)
        for i in range(PER_KV):
            out_ref[side * s : side * (s + 1), i * HD : (i + 1) * HD] = result[side * i : side * (i + 1)]

    for copy in first:
        copy.wait_send()
    for g in range(4):
        sent = picked.at[g, pl.ds(0, OWNERS - 1)]
        pltpu.make_async_copy(sent, sent, s2.at[g]).wait()


def local(prompt_kv, prompt_lengths, owner_prompts, owner_counts, queries, new_kv):
    smem, any_space = pl.BlockSpec(memory_space=pltpu.SMEM), pl.BlockSpec(memory_space=pl.ANY)
    vmem = pl.BlockSpec(memory_space=pltpu.VMEM)
    bf16, f32 = jnp.bfloat16, jnp.float32
    result = pl.pallas_call(
        kernel,
        out_shape=jax.ShapeDtypeStruct((GROUP * SLOTS * STEPS, PER_KV * HD), bf16),
        in_specs=[smem, smem, smem, vmem, any_space, any_space, any_space],
        out_specs=vmem,
        scratch_shapes=[
            pltpu.VMEM(prompt_kv.shape, bf16),
            pltpu.VMEM(queries.shape, bf16),
            pltpu.VMEM(new_kv.shape, bf16),
            pltpu.VMEM((PROMPTS * POS, 2048), f32),
            pltpu.VMEM((HEADS, PROMPTS * POS, 2 * HD), bf16),
            pltpu.VMEM((4, 2, PROMPTS * POS, 2 * HD), bf16),
            pltpu.VMEM((4, OWNERS, 16, HD), bf16),
            pltpu.VMEM((4, OWNERS, 16, HD), bf16),
            pltpu.VMEM((OWNERS * 8, 2 * PROMPTS * POS), bf16),
            pltpu.VMEM((256, 256), bf16),
            pltpu.VMEM((SLOTS, HD, 512), bf16),
            pltpu.VMEM((8, 512), f32),
            pltpu.VMEM((8, 512), f32),
            pltpu.VMEM((SLOTS, HD, 512), f32),
            pltpu.SemaphoreType.DMA((3,)),
            pltpu.SemaphoreType.DMA((7,)),
            pltpu.SemaphoreType.DMA((4,)),
            pltpu.SemaphoreType.DMA((4,)),
            pltpu.SemaphoreType.DMA((4,)),
        ],
        compiler_params=pltpu.CompilerParams(
            collective_id=0, has_side_effects=True, vmem_limit_bytes=32 << 20
        ),
        cost_estimate=pl.CostEstimate(flops=10**9, bytes_accessed=3 << 20, transcendentals=1 << 20),
    )(prompt_lengths, owner_prompts, owner_counts, owner_prompts, prompt_kv, queries, new_kv)
    return result.reshape(queries.shape)


def solution(mesh):
    return jax.shard_map(
        local,
        mesh=mesh,
        in_specs=(
            P(None, ("head", "batch"), None),
            P(),
            P(),
            P("batch"),
            P("batch", None, "head"),
            P("batch", None, "head"),
        ),
        out_specs=P("batch", None, "head"),
        check_vma=False,
    )
```

time: 140 us -> 63 us (0.45)
  blocking collectives: 66.7 us -> 0 us
  Pallas kernels: 0 us -> 57.8 us
  waiting for transfers between devices: 24.4 us -> 0 us
  local copies, waits for them, and re-layouts: 24.9 us -> 4.29 us
  starting transfers between devices: 12.1 us -> 0 us
  matrix products: 5.21 us -> 0 us
  other arithmetic: 5.11 us -> 0 us
    all_to_all x1 -> x0, blocking collectives: 66.7 us -> none  [local(): lax.all_to_all(outgoing, 'head', split_axis=3, concat_axis=2, tiled=True)]
    pallas_call x0 -> x1, Pallas kernels: none -> 57.8 us  [local(): pl.pallas_call(kernel, out_shape=jax.ShapeDtypeStruct((GROUP * SLOTS * ST...]
    all_to_all x1 -> x0, waiting for transfers between devices: 24.4 us -> none  [local(): lax.all_to_all(regrouped, 'batch', split_axis=0, concat_axis=2, tiled=True)]
    all_to_all x1 -> x0, starting transfers between devices: 12.1 us -> none  [local(): lax.all_to_all(regrouped, 'batch', split_axis=0, concat_axis=2, tiled=True)]
    all_to_all x3 -> x0, local copies, waits for them, and re-layouts: 7.1 us -> none  [the longest x2 7.02 us: local(): lax.all_to_all(outgoing, 'head', split_axis=3, concat_axis=2, tiled=True)]
    dot_general x4 -> x0, matrix products: 5.21 us -> none  [the longest x1 2.72 us: step_block(): jnp.einsum('kgtjqn,knjd->kgtjqd', exps.astype(jnp.bfloat16), keys_view[:,...]
    select_n x2 -> x0, local copies, waits for them, and re-layouts: 4.98 us -> none  [local(): outgoing = jnp.take(prompt_kv, owner_prompts, axis=0)]
    select_n x2 -> x0, other arithmetic: 2.8 us -> none  [local(): outgoing = jnp.take(prompt_kv, owner_prompts, axis=0)]
  transfers between devices with their start and end apart: 1 -> 0, of which waited for: 1 -> 0; matrix products, arithmetic and copies ran while one was open for 2% -> 0% of each run, Pallas kernels for 0% -> 0%
where the time goes in v1:
time: 63 us; the launch traced here: 62.7 us
  Pallas kernels  57.8 us (92%)
  local copies, waits for them, and re-layouts  4.29 us (7%)
  between operations  0.69 us (1%)
    pallas_call x1, Pallas kernels, local(): pl.pallas_call(kernel, out_shape=jax.ShapeDtypeStruct((GROUP * SLOTS * ST...  57.8 us
    unnamed x11, local copies, waits for them, and re-layouts  3.49 us

profile of v1, /device:TPU:1, one launch (start us, length us, event | category | flops | bytes accessed | tf_op | source)
XLA Modules:
  0.0 62.7 jit_solution(12432112387353032997)
XLA Ops:
  0.0 0.0 copy-start.4
  0.7 0.0 copy-done.4
  0.7 0.0 copy-start.3
  0.7 0.1 copy.7.prompts.prompts_v
  0.8 0.6 copy-done.3
  1.3 0.0 copy-start
  1.3 1.0 %copy-done = bf16[64,2,2048]{2,1,0:T(2,128)(2,1)S(1)} copy-done((bf16[64,2,2048]{2,1,0:T(2,128)(2,1)S(1)}, bf16[64,2,2048]{2,1,0:T(2,128)(2,1)}, u32[]{:S(2)}) %copy-start) | copy-done | bytes 524312
  2.4 0.0 copy-start.1
  2.4 0.9 %copy-done.1 = bf16[32,4,1024]{2,1,0:T(4,128)(2,1)S(1)} copy-done((bf16[32,4,1024]{2,1,0:T(4,128)(2,1)S(1)}, bf16[32,4,1024]{2,1,0:T(4,128)(2,1)}, u32[]{:S(2)}) %copy-start.1) | copy-done | bytes 262168
  3.3 0.0 copy-start.2
  3.3 0.8 %copy-done.2 = bf16[32,4,256]{2,1,0:T(4,128)(2,1)S(1)} copy-done((bf16[32,4,256]{2,1,0:T(4,128)(2,1)S(1)}, bf16[32,4,256]{2,1,0:T(4,128)(2,1)}, u32[]{:S(2)}) %copy-start.2) | copy-done | bytes 65560
  4.2 57.8 %shard_map.64 = bf16[128,1024]{1,0:T(8,128)(2,1)S(1)} custom-call(s32[64]{0:T(128)S(1)} %copy-done.3, s32[64,2]{1,0:T(8,128)S(1)} %copy.7.prompts.prompts_v, s32[1]{0:T(128)S(6)} %copy.9.counts, s32[64,2]{1,0:T(8,128)S(1)} %copy.7.prompts.prompts_v, bf16[64,2,2048]{2,1,0:T(2,128)(2,1)S(1)} %copy-done, bf16[32,4,1024]{2,1,0:T(4,128)(2,1)S(1)} %copy-done.1, ...), custom_call_target="tpu_custom_call" | custom-call | flops 1000000000 | bytes 3145728 | tf_op jit(solution)/shard_map/pallas_call | solution.py:202
  61.9 0.8 %reshape.3 = bf16[32,4,1024]{2,1,0:T(4,128)(2,1)} reshape(bf16[128,1024]{1,0:T(8,128)(2,1)S(1)} %shard_map.64) | data formatting | bytes 524288 | tf_op jit(solution)/shard_map/reshape | solution.py:233
Async XLA Ops:
  0.0 0.7 %copy-start.4 = (s32[64,2]{0,1:T(2,128)S(1)}, s32[64,2]{0,1:T(2,128)}, u32[]{:S(2)}) copy-start(s32[64,2]{0,1:T(2,128)} %param.8) | copy-start | bytes 1540
  0.7 0.7 %copy-start.3 = (s32[64]{0:T(128)S(1)}, s32[64]{0:T(128)}, u32[]{:S(2)}) copy-start(s32[64]{0:T(128)} %lengths.1) | copy-start | bytes 772
  1.3 1.0 %copy-start = (bf16[64,2,2048]{2,1,0:T(2,128)(2,1)S(1)}, bf16[64,2,2048]{2,1,0:T(2,128)(2,1)}, u32[]{:S(2)}) copy-start(bf16[64,2,2048]{2,1,0:T(2,128)(2,1)} %kv_hbm.1) | copy-start | bytes 1572868
  2.4 0.9 %copy-start.1 = (bf16[32,4,1024]{2,1,0:T(4,128)(2,1)S(1)}, bf16[32,4,1024]{2,1,0:T(4,128)(2,1)}, u32[]{:S(2)}) copy-start(bf16[32,4,1024]{2,1,0:T(4,128)(2,1)} %q_hbm.1) | copy-start | bytes 786436
  3.3 0.8 %copy-start.2 = (bf16[32,4,256]{2,1,0:T(4,128)(2,1)S(1)}, bf16[32,4,256]{2,1,0:T(4,128)(2,1)}, u32[]{:S(2)}) copy-start(bf16[32,4,256]{2,1,0:T(4,128)(2,1)} %new_hbm.1) | copy-start | bytes 196612

commit v2 on v1

--- a/solution.py
+++ b/solution.py
@@ -56,13 +56,15 @@
     return run + 2, jnp.where(upper, odd, 2 + odd)
 
 
-def kernel(lengths, prompts, counts, prompts_v, kv_hbm, q_hbm, new_hbm, out_ref,
-           kv, q, new, wide, send, land, picked, got, pick, sort, qt, top, total, acc,
+def kernel(lengths_hbm, prompts_hbm, counts_hbm, kv_hbm, q_hbm, new_hbm, out_ref,
+           lengths, prompts, counts, prompts_v, kv, q, new, wide, send, land, picked, got, pick, sort, qt, top, total, acc,
            in_sem, s1, r1, s2, r2):
     run, core, yx, node = place()
     me_head, me = lax.axis_index("head"), lax.axis_index("batch")
 
-    loads = [pltpu.make_async_copy(a, b, in_sem.at[i]) for i, (a, b) in enumerate(((kv_hbm, kv), (q_hbm, q), (new_hbm, new)))]
+    pairs = ((kv_hbm, kv), (prompts_hbm, prompts_v), (prompts_hbm, prompts), (lengths_hbm, lengths),
+             (counts_hbm, counts), (q_hbm, q), (new_hbm, new))
+    loads = [pltpu.make_async_copy(a, b, in_sem.at[i]) for i, (a, b) in enumerate(pairs)]
     for load in loads:
         load.start()
 
@@ -85,7 +87,10 @@
 
     rows, cols = OWNERS * 8, 2 * PROMPTS * POS
     owner_hot = (iota((rows, OWNERS), 0) // 8 == iota((rows, OWNERS), 1)).astype(jnp.bfloat16)
-    ids = jnp.dot(owner_hot, prompts_v[...].astype(jnp.float32).astype(jnp.bfloat16), preferred_element_type=jnp.float32)
+    loads[1].wait()
+    ids = lax.dot_general(
+        owner_hot, prompts_v[...].astype(jnp.float32).astype(jnp.bfloat16), (((1,), (1,)), ((), ())),
+        preferred_element_type=jnp.float32)
     r1d = iota((rows, 1), 0)
     ids = jnp.where(r1d // 4 % 2 == 0, ids[:, 0:1], ids[:, 1:2]).astype(jnp.int32)
     want = (r1d // 2 % 2) * (PROMPTS * POS) + ids * POS + r1d % 2
@@ -124,8 +129,8 @@
 
     relay(0)
 
-    loads[1].wait()
-    loads[2].wait()
+    for load in loads[2:]:
+        load.wait()
     for g in range(GROUP * SLOTS):
         wide[STEPS * g : STEPS * (g + 1), :1024] = q[g].astype(jnp.float32)
         wide[STEPS * g : STEPS * (g + 1), 1024:1280] = new[g].astype(jnp.float32)
@@ -169,7 +174,7 @@
             keys = jnp.concatenate([b[64 * s : 64 * (s + 1)] for b in blocks], axis=0)
             values = jnp.concatenate([b[128 + 64 * s : 128 + 64 * (s + 1)] for b in blocks], axis=0)
             scores = jnp.dot(keys, qt[s], preferred_element_type=jnp.float32) * SCALE
-            scores = jnp.where(position < lengths[prompts[me, s]], scores, LOWEST)
+            scores = jnp.where(position < lengths[prompts[s, me]], scores, LOWEST)
             before = top[s : s + 1, :]
             m = jnp.maximum(before, jnp.max(scores, axis=0, keepdims=True))
             e = jnp.exp2(scores - m)
@@ -196,15 +201,18 @@
 
 
 def local(prompt_kv, prompt_lengths, owner_prompts, owner_counts, queries, new_kv):
-    smem, any_space = pl.BlockSpec(memory_space=pltpu.SMEM), pl.BlockSpec(memory_space=pl.ANY)
-    vmem = pl.BlockSpec(memory_space=pltpu.VMEM)
+    hbm, vmem = pl.BlockSpec(memory_space=pltpu.HBM), pl.BlockSpec(memory_space=pltpu.VMEM)
     bf16, f32 = jnp.bfloat16, jnp.float32
     result = pl.pallas_call(
         kernel,
         out_shape=jax.ShapeDtypeStruct((GROUP * SLOTS * STEPS, PER_KV * HD), bf16),
-        in_specs=[smem, smem, smem, vmem, any_space, any_space, any_space],
+        in_specs=[hbm] * 6,
         out_specs=vmem,
         scratch_shapes=[
+            pltpu.SMEM(prompt_lengths.shape, jnp.int32),
+            pltpu.SMEM((SLOTS, OWNERS), jnp.int32),
+            pltpu.SMEM(owner_counts.shape, jnp.int32),
+            pltpu.VMEM((SLOTS, OWNERS), jnp.int32),
             pltpu.VMEM(prompt_kv.shape, bf16),
             pltpu.VMEM(queries.shape, bf16),
             pltpu.VMEM(new_kv.shape, bf16),
@@ -219,17 +227,17 @@
             pltpu.VMEM((8, 512), f32),
             pltpu.VMEM((8, 512), f32),
             pltpu.VMEM((SLOTS, HD, 512), f32),
-            pltpu.SemaphoreType.DMA((3,)),
+            pltpu.SemaphoreType.DMA((7,)),
             pltpu.SemaphoreType.DMA((7,)),
             pltpu.SemaphoreType.DMA((4,)),
             pltpu.SemaphoreType.DMA((4,)),
             pltpu.SemaphoreType.DMA((4,)),
         ],
         compiler_params=pltpu.CompilerParams(
-            collective_id=0, has_side_effects=True, vmem_limit_bytes=32 << 20
+            collective_id=0, has_side_effects=True, vmem_limit_bytes=60 << 20
         ),
         cost_estimate=pl.CostEstimate(flops=10**9, bytes_accessed=3 << 20, transcendentals=1 << 20),
-    )(prompt_lengths, owner_prompts, owner_counts, owner_prompts, prompt_kv, queries, new_kv)
+    )(prompt_lengths, owner_prompts.T, owner_counts, prompt_kv, queries, new_kv)
     return result.reshape(queries.shape)
 
 

time: 63 us -> 59.9 us (0.951)
  local copies, waits for them, and re-layouts: 4.29 us -> 1.76 us
    unnamed x11 -> x0, local copies, waits for them, and re-layouts: 3.49 us -> none
    reshape x1, local copies, waits for them, and re-layouts: 0.8 us -> 1.76 us  [local(): return result.reshape(queries.shape)]
where the time goes in v2:
time: 59.9 us; the launch traced here: 59.7 us
  Pallas kernels  57.3 us (96%)
  local copies, waits for them, and re-layouts  1.76 us (3%)
  between operations  0.66 us (1%)
    pallas_call x1, Pallas kernels, local(): pl.pallas_call(kernel, out_shape=jax.ShapeDtypeStruct((GROUP * SLOTS * ST...  57.3 us
    reshape x1, local copies, waits for them, and re-layouts, local(): return result.reshape(queries.shape)  1.76 us

profile of v2, /device:TPU:1, one launch (start us, length us, event | category | flops | bytes accessed | tf_op | source)
XLA Modules:
  0.0 59.7 jit_solution(11630249856656052229)
XLA Ops:
  0.7 57.3 %shard_map.64 = bf16[128,1024]{1,0:T(8,128)(2,1)} custom-call(s32[64]{0:T(128)} %lengths_hbm.1, s32[2,64]{1,0:T(2,128)} %bitcast.1, s32[1]{0:T(128)S(6)} %copy.7.counts_hbm, bf16[64,2,2048]{2,1,0:T(2,128)(2,1)} %kv_hbm.1, bf16[32,4,1024]{2,1,0:T(4,128)(2,1)} %q_hbm.1, bf16[32,4,256]{2,1,0:T(4,128)(2,1)} %new_hbm.1), custom_call_target="tpu_custom_call" | custom-call | flops 1000000000 | bytes 3145728 | tf_op jit(solution)/shard_map/pallas_call | solution.py:206
  57.9 1.8 %reshape.3 = bf16[32,4,1024]{2,1,0:T(4,128)(2,1)} reshape(bf16[128,1024]{1,0:T(8,128)(2,1)} %shard_map.64) | data formatting | bytes 524288 | tf_op jit(solution)/shard_map/reshape | solution.py:241

commit v3 on v2

--- a/solution.py
+++ b/solution.py
@@ -56,14 +56,14 @@
     return run + 2, jnp.where(upper, odd, 2 + odd)
 
 
-def kernel(lengths_hbm, prompts_hbm, counts_hbm, kv_hbm, q_hbm, new_hbm, out_ref,
-           lengths, prompts, counts, prompts_v, kv, q, new, wide, send, land, picked, got, pick, sort, qt, top, total, acc,
+def kernel(lengths_hbm, prompts_hbm, counts, kv_hbm, q_hbm, new_hbm, out_ref,
+           lengths, prompts, prompts_v, kv, q, new, wide, send, land, picked, got, pick, sort, qt, top, total, acc,
            in_sem, s1, r1, s2, r2):
     run, core, yx, node = place()
     me_head, me = lax.axis_index("head"), lax.axis_index("batch")
 
     pairs = ((kv_hbm, kv), (prompts_hbm, prompts_v), (prompts_hbm, prompts), (lengths_hbm, lengths),
-             (counts_hbm, counts), (q_hbm, q), (new_hbm, new))
+             (q_hbm, q), (new_hbm, new))
     loads = [pltpu.make_async_copy(a, b, in_sem.at[i]) for i, (a, b) in enumerate(pairs)]
     for load in loads:
         load.start()
@@ -107,7 +107,7 @@
     for hop in (1, 2, 3):
         to_run, to_node = relay_of(hop)
         for k in (0, 1):
-            to = device(to_run, k, yx, to_node)
+            to = device(to_run, lax.rem(core + k, 2), yx, to_node)
             first.append(pltpu.make_async_remote_copy(
                 send.at[to[0]], land.at[hop, core], s1.at[2 * hop - 1 + k], r1.at[hop], device_id=to, device_id_type=MESH))
     for copy in first:
@@ -200,18 +200,21 @@
         pltpu.make_async_copy(sent, sent, s2.at[g]).wait()
 
 
+def stay(x):
+    return pltpu.with_memory_space_constraint(x, pltpu.HBM)
+
+
 def local(prompt_kv, prompt_lengths, owner_prompts, owner_counts, queries, new_kv):
     hbm, vmem = pl.BlockSpec(memory_space=pltpu.HBM), pl.BlockSpec(memory_space=pltpu.VMEM)
     bf16, f32 = jnp.bfloat16, jnp.float32
     result = pl.pallas_call(
         kernel,
-        out_shape=jax.ShapeDtypeStruct((GROUP * SLOTS * STEPS, PER_KV * HD), bf16),
-        in_specs=[hbm] * 6,
+        out_shape=pltpu.VMEM((GROUP * SLOTS * STEPS, PER_KV * HD), bf16),
+        in_specs=[hbm, hbm, pl.BlockSpec(memory_space=pltpu.SMEM), hbm, hbm, hbm],
         out_specs=vmem,
         scratch_shapes=[
             pltpu.SMEM(prompt_lengths.shape, jnp.int32),
             pltpu.SMEM((SLOTS, OWNERS), jnp.int32),
-            pltpu.SMEM(owner_counts.shape, jnp.int32),
             pltpu.VMEM((SLOTS, OWNERS), jnp.int32),
             pltpu.VMEM(prompt_kv.shape, bf16),
             pltpu.VMEM(queries.shape, bf16),
@@ -227,17 +230,17 @@
             pltpu.VMEM((8, 512), f32),
             pltpu.VMEM((8, 512), f32),
             pltpu.VMEM((SLOTS, HD, 512), f32),
-            pltpu.SemaphoreType.DMA((7,)),
+            pltpu.SemaphoreType.DMA((6,)),
             pltpu.SemaphoreType.DMA((7,)),
             pltpu.SemaphoreType.DMA((4,)),
             pltpu.SemaphoreType.DMA((4,)),
             pltpu.SemaphoreType.DMA((4,)),
         ],
         compiler_params=pltpu.CompilerParams(
-            collective_id=0, has_side_effects=True, vmem_limit_bytes=60 << 20
+            collective_id=0, has_side_effects=True, vmem_limit_bytes=48 << 20
         ),
         cost_estimate=pl.CostEstimate(flops=10**9, bytes_accessed=3 << 20, transcendentals=1 << 20),
-    )(prompt_lengths, owner_prompts.T, owner_counts, prompt_kv, queries, new_kv)
+    )(stay(prompt_lengths), stay(owner_prompts.T), owner_counts, stay(prompt_kv), stay(queries), stay(new_kv))
     return result.reshape(queries.shape)
 
 

time: 59.9 us -> 58 us (0.968)
  local copies, waits for them, and re-layouts: 1.76 us -> 0.8 us
  Pallas kernels: 57.3 us -> 56.4 us
    reshape x1, local copies, waits for them, and re-layouts: 1.76 us -> 0.8 us  [local(): return result.reshape(queries.shape)]
    pallas_call x1, Pallas kernels: 57.3 us -> 56.4 us  [local(): pl.pallas_call(kernel, out_shape=pltpu.VMEM((GROUP * SLOTS * STEPS, PER_K...]
where the time goes in v3:
time: 58 us; the launch traced here: 57.9 us
  Pallas kernels  56.4 us (97%)
  local copies, waits for them, and re-layouts  0.8 us (1%)
  between operations  0.66 us (1%)
    pallas_call x1, Pallas kernels, local(): pl.pallas_call(kernel, out_shape=pltpu.VMEM((GROUP * SLOTS * STEPS, PER_K...  56.4 us

profile of v3, /device:TPU:1, one launch (start us, length us, event | category | flops | bytes accessed | tf_op | source)
XLA Modules:
  0.0 57.9 jit_solution(5891068208362944187)
XLA Ops:
  0.7 56.4 %shard_map.64 = bf16[128,1024]{1,0:T(8,128)(2,1)S(1)} custom-call(s32[64]{0:T(128)} %lengths_hbm.1, s32[2,64]{1,0:T(2,128)} %bitcast.1, s32[1]{0:T(128)S(6)} %copy.7.counts, bf16[64,2,2048]{2,1,0:T(2,128)(2,1)} %kv_hbm.1, bf16[32,4,1024]{2,1,0:T(4,128)(2,1)} %q_hbm.1, bf16[32,4,256]{2,1,0:T(4,128)(2,1)} %new_hbm.1), custom_call_target="tpu_custom_call" | custom-call | flops 1000000000 | bytes 3145728 | tf_op jit(solution)/shard_map/pallas_call | solution.py:210
  57.1 0.8 %reshape.3 = bf16[32,4,1024]{2,1,0:T(4,128)(2,1)} reshape(bf16[128,1024]{1,0:T(8,128)(2,1)S(1)} %shard_map.64) | data formatting | bytes 524288 | tf_op jit(solution)/shard_map/reshape | solution.py:244

commit v4 on v3

--- a/solution.py
+++ b/solution.py
@@ -39,21 +39,19 @@
     run, _, _, node = place()
     odd, upper = node % 2, node // 2 == 1
     if hop == 1:
-        return jnp.where(upper, run + 1, run + 3), jnp.where(upper, odd, 2 + odd)
+        return jnp.where(upper, run + 1, run + 3), jnp.where(upper, 0, 3), jnp.where(upper, 2 - odd, 1 + odd)
     if hop == 2:
-        return jnp.where(upper, run + 3, run + 1), jnp.where(upper, 2 + odd, odd)
-    return run + 2, jnp.where(upper, odd, 2 + odd)
-
-
-def source_of(hop, run, node):
-    odd, upper = node % 2, node // 2 == 1
-    if hop == 0:
+        return jnp.where(upper, run + 3, run + 1), jnp.where(upper, 2, 1), jnp.where(upper, 1 + odd, 2 - odd)
+    return run + 2, jnp.where(upper, odd, 2 + odd), 3
+
+
+def source_of(group, run, node):
+    if group == 0:
         return run + 0 * node, node
-    if hop == 1:
-        return jnp.where(upper, run + 1, run + 3), jnp.where(upper, odd, 2 + odd)
-    if hop == 2:
-        return jnp.where(upper, run + 1, run + 3), jnp.where(upper, 2 + odd, odd)
-    return run + 2, jnp.where(upper, odd, 2 + odd)
+    if group == 3:
+        return run + 2 + 0 * node, (node + 2) % 4
+    left = node < 2
+    return jnp.where(left, run + 3, run + 1), jnp.where(left, 4 - group, 5 + group) - 2 * node
 
 
 def kernel(lengths_hbm, prompts_hbm, counts, kv_hbm, q_hbm, new_hbm, out_ref,
@@ -69,8 +67,8 @@
         load.start()
 
     barrier = pltpu.get_barrier_semaphore()
-    for hop in (3, 2, 1):
-        their_run, their_node = source_of(hop, run, node)
+    for group in (3, 2, 1):
+        their_run, their_node = source_of(group, run, node)
         for k in (0, 1):
             pl.semaphore_signal(barrier, inc=1, device_id=device(their_run, k, yx, their_node), device_id_type=MESH)
     pl.semaphore_signal(barrier, inc=1, device_id=device(run, 1 - core, yx, node), device_id_type=MESH)
@@ -105,11 +103,11 @@
         send.at[run * 2 + 1 - core], land.at[0, core], s1.at[0], r1.at[0],
         device_id=device(run, 1 - core, yx, node), device_id_type=MESH))
     for hop in (1, 2, 3):
-        to_run, to_node = relay_of(hop)
+        to_run, to_node, group = relay_of(hop)
         for k in (0, 1):
             to = device(to_run, lax.rem(core + k, 2), yx, to_node)
             first.append(pltpu.make_async_remote_copy(
-                send.at[to[0]], land.at[hop, core], s1.at[2 * hop - 1 + k], r1.at[hop], device_id=to, device_id_type=MESH))
+                send.at[to[0]], land.at[group, core], s1.at[2 * hop - 1 + k], r1.at[group], device_id=to, device_id_type=MESH))
     for copy in first:
         copy.start()
 

time: 58 us -> 56.9 us (0.981)
  Pallas kernels: 56.4 us -> 55.3 us
    pallas_call x1, Pallas kernels: 56.4 us -> 55.3 us  [local(): pl.pallas_call(kernel, out_shape=pltpu.VMEM((GROUP * SLOTS * STEPS, PER_K...]
where the time goes in v4:
time: 56.9 us; the launch traced here: 56.8 us
  Pallas kernels  55.3 us (97%)
  local copies, waits for them, and re-layouts  0.8 us (1%)
  between operations  0.66 us (1%)
    pallas_call x1, Pallas kernels, local(): pl.pallas_call(kernel, out_shape=pltpu.VMEM((GROUP * SLOTS * STEPS, PER_K...  55.3 us

profile of v4, /device:TPU:1, one launch (start us, length us, event | category | flops | bytes accessed | tf_op | source)
XLA Modules:
  0.0 56.8 jit_solution(12281439561944965571)
XLA Ops:
  0.7 55.3 %shard_map.64 = bf16[128,1024]{1,0:T(8,128)(2,1)S(1)} custom-call(s32[64]{0:T(128)} %lengths_hbm.1, s32[2,64]{1,0:T(2,128)} %bitcast.1, s32[1]{0:T(128)S(6)} %copy.7.counts, bf16[64,2,2048]{2,1,0:T(2,128)(2,1)} %kv_hbm.1, bf16[32,4,1024]{2,1,0:T(4,128)(2,1)} %q_hbm.1, bf16[32,4,256]{2,1,0:T(4,128)(2,1)} %new_hbm.1), custom_call_target="tpu_custom_call" | custom-call | flops 1000000000 | bytes 3145728 | tf_op jit(solution)/shard_map/pallas_call | solution.py:208
  56.0 0.8 %reshape.3 = bf16[32,4,1024]{2,1,0:T(4,128)(2,1)} reshape(bf16[128,1024]{1,0:T(8,128)(2,1)S(1)} %shard_map.64) | data formatting | bytes 524288 | tf_op jit(solution)/shard_map/reshape | solution.py:242

commit v5 on v4

--- a/solution.py
+++ b/solution.py
@@ -157,22 +157,23 @@
     relay(3)
 
     def attend(g):
+        n = iota((256, 1), 0)
+        relay_id = n // 4
+        from_run, from_node = source_of(g, run, relay_id % 4)
+        from_head = lax.rem(from_run + RUNS, RUNS) * 2 + n // 2 % 2
+        position = (from_head * OWNERS + relay_id // 4 * 4 + from_node) * POS + n % 2
+        inside = [position < lengths[prompts[s, me]] for s in range(SLOTS)]
         pltpu.make_async_copy(got.at[g], got.at[g], r2.at[g]).wait()
         flat = got[g].reshape(OWNERS * 16, HD)
         blocks = [
             jnp.dot(sort[...], flat[256 * i : 256 * (i + 1)], preferred_element_type=jnp.float32).astype(jnp.bfloat16)
             for i in range(4)
         ]
-        n = iota((256, rows), 0)
-        relay_id = n // 4
-        from_run, from_node = source_of(g, run, relay_id % 4)
-        from_head = lax.rem(from_run + RUNS, RUNS) * 2 + n // 2 % 2
-        position = (from_head * OWNERS + relay_id // 4 * 4 + from_node) * POS + n % 2
         for s in range(SLOTS):
             keys = jnp.concatenate([b[64 * s : 64 * (s + 1)] for b in blocks], axis=0)
             values = jnp.concatenate([b[128 + 64 * s : 128 + 64 * (s + 1)] for b in blocks], axis=0)
             scores = jnp.dot(keys, qt[s], preferred_element_type=jnp.float32) * SCALE
-            scores = jnp.where(position < lengths[prompts[s, me]], scores, LOWEST)
+            scores = jnp.where(inside[s], scores, LOWEST)
             before = top[s : s + 1, :]
             m = jnp.maximum(before, jnp.max(scores, axis=0, keepdims=True))
             e = jnp.exp2(scores - m)
@@ -187,7 +188,7 @@
 
     for s in range(SLOTS):
         live = s * GROUP < counts[0]
-        result = jnp.where(live, acc[s] / total[s : s + 1, :], 0.0).T.astype(jnp.bfloat16)
+        result = (acc[s] * jnp.where(live, 1.0 / total[s : s + 1, :], 0.0)).T.astype(jnp.bfloat16)
         for i in range(PER_KV):
             out_ref[side * s : side * (s + 1), i * HD : (i + 1) * HD] = result[side * i : side * (i + 1)]
 

time: 56.9 us -> 56.9 us (level)
  no operation moved by 1% of the time
where the time goes in v5:
time: 56.9 us; the launch traced here: 56.8 us
  Pallas kernels  55.3 us (97%)
  local copies, waits for them, and re-layouts  0.8 us (1%)
  between operations  0.66 us (1%)
    pallas_call x1, Pallas kernels, local(): pl.pallas_call(kernel, out_shape=pltpu.VMEM((GROUP * SLOTS * STEPS, PER_K...  55.3 us

profile of v5, /device:TPU:1, one launch (start us, length us, event | category | flops | bytes accessed | tf_op | source)
XLA Modules:
  0.0 56.8 jit_solution(12818667027808519370)
XLA Ops:
  0.7 55.3 %shard_map.64 = bf16[128,1024]{1,0:T(8,128)(2,1)S(1)} custom-call(s32[64]{0:T(128)} %lengths_hbm.1, s32[2,64]{1,0:T(2,128)} %bitcast.1, s32[1]{0:T(128)S(6)} %copy.7.counts, bf16[64,2,2048]{2,1,0:T(2,128)(2,1)} %kv_hbm.1, bf16[32,4,1024]{2,1,0:T(4,128)(2,1)} %q_hbm.1, bf16[32,4,256]{2,1,0:T(4,128)(2,1)} %new_hbm.1), custom_call_target="tpu_custom_call" | custom-call | flops 1000000000 | bytes 3145728 | tf_op jit(solution)/shard_map/pallas_call | solution.py:209
  56.0 0.8 %reshape.3 = bf16[32,4,1024]{2,1,0:T(4,128)(2,1)} reshape(bf16[128,1024]{1,0:T(8,128)(2,1)S(1)} %shard_map.64) | data formatting | bytes 524288 | tf_op jit(solution)/shard_map/reshape | solution.py:243
